TPU v7x, 32 devices: a whole 2x2x4 slice. The times are simulated.
32 devices in a mesh: groups: 2 (over y), seq: 16 (over z, x, core).
Axes of the slice: x: 2, y: 2, z: 4, core: 2. Of those that a mesh axis runs over, the one named last changes fastest.
Arguments:
- inputs: float32 [2048, 128], P(('groups', 'seq')), parts along dimension 0, may hold values from -6 to 6
- guesses: float32 [2048, 128], P(('groups', 'seq')), parts along dimension 0, may hold values from -3 to 3
- initial: float32 [256], P('groups'), parts along dimension 0, may hold values from -4 to 4
- w_input: float32 [128, 384], replicated, may hold values from -0.5 to 0.5
- w_hidden: float32 [128, 384], replicated, may hold values from -0.5 to 0.5
- biases: float32 [384], replicated, as said below
Outputs:
- trajectory: float32 [2048, 128], P(('groups', 'seq')), parts along dimension 0
There are 2 independent parts, one for each index of `groups`. A program takes and returns all parts, laid end to end along the dimension named above; an argument that names none is the same for every part. Nothing has to cross between parts.
Inputs may be any that keep to these rules, and one draw needn't show every extreme that they name: Entries 0 to 127 are the update gate's biases, the others those of the reset gate and the candidate.
All inputs are finite; a program needn't handle non-finite values.
Results may differ from a plain program's by a relative error of at most 0.0004.
Values sent between devices are 32-bit elements; how exact they have to be, the bound alone decides.
A program may use at most 128 MiB of HBM per device.

v0:
```python
import jax
import jax.numpy as jnp
from jax import lax
from jax.sharding import PartitionSpec as P


def passed_along(value, axis, steps):
    count = lax.axis_size(axis)
    initial, last = (max(0, -steps), min(count, count - steps))
    return lax.ppermute(value, axis, [(source, source + steps) for source in range(initial, last)])


def coefficients(previous, pre, rec, width):
    pz, pr, pn = (pre[:, :width], pre[:, width : 2 * width], pre[:, 2 * width :])
    cz, cr, cn = (rec[:, :width], rec[:, width : 2 * width], rec[:, 2 * width :])
    update = jax.nn.sigmoid(pz + cz)
    reset = jax.nn.sigmoid(pr + cr)
    cand = jnp.tanh(pn + reset * cn)
    value = (1.0 - update) * cand + update * previous
    coef_update = (previous - cand) * update * (1.0 - update)
    coef_cand = (1.0 - update) * (1.0 - cand * cand) * reset
    coef_reset = (1.0 - update) * (1.0 - cand * cand) * cn * reset * (1.0 - reset)
    offset = value - (update * previous + coef_update * cz + coef_cand * cn + coef_reset * cr)
    return (update, coef_update, coef_cand, coef_reset, offset)


def compose(earlier, later):
    map_early, shift_early = earlier
    map_late, shift_late = later
    new_map = jnp.einsum("...ki,...ij->...kj", map_early, map_late, precision=lax.Precision.HIGHEST)
    new_shift = (
        jnp.einsum("...i,...ij->...j", shift_early, map_late, precision=lax.Precision.HIGHEST)
        + shift_late
    )
    return (new_map, new_shift)


def per_device(inputs, guesses, initial, w_input, w_hidden, biases):
    width = guesses.shape[1]
    position = lax.axis_index("seq")
    before = passed_along(guesses[-1:], "seq", 1)
    first_row = jnp.where(position == 0, initial[None, :], before)
    previous = jnp.concatenate([first_row, guesses[:-1]], axis=0)
    pre = (
        jnp.dot(
            inputs, w_input, precision=lax.Precision.HIGHEST, preferred_element_type=jnp.float32
        )
        + biases
    )
    rec = jnp.dot(
        previous, w_hidden, precision=lax.Precision.HIGHEST, preferred_element_type=jnp.float32
    )
    update, coef_update, coef_cand, coef_reset, offset = coefficients(previous, pre, rec, width)
    identity = jnp.eye(width, dtype=jnp.float32)
    step_maps = (
        update[:, None, :] * identity[None]
        + coef_update[:, None, :] * w_hidden[None, :, :width]
        + coef_reset[:, None, :] * w_hidden[None, :, width : 2 * width]
        + coef_cand[:, None, :] * w_hidden[None, :, 2 * width :]
    )
    prefix_maps, prefix_shifts = lax.associative_scan(compose, (step_maps, offset))
    total_map = prefix_maps[-1]
    total_shift = prefix_shifts[-1]
    every_map, every_shift = (
        lax.all_gather(total_map[None], "seq", axis=0, tiled=True),
        lax.all_gather(total_shift[None], "seq", axis=0, tiled=True),
    )
    running_maps, running_shifts = lax.associative_scan(compose, (every_map, every_shift))
    earlier_num = jnp.maximum(position - 1, 0)
    chosen_map = lax.dynamic_index_in_dim(running_maps, earlier_num, 0, keepdims=False)
    chosen_shift = lax.dynamic_index_in_dim(running_shifts, earlier_num, 0, keepdims=False)
    moved = (
        jnp.dot(
            initial, chosen_map, precision=lax.Precision.HIGHEST, preferred_element_type=jnp.float32
        )
        + chosen_shift
    )
    entry_state = jnp.where(position > 0, moved, initial)
    trajectory = (
        jnp.einsum("k,tkj->tj", entry_state, prefix_maps, precision=lax.Precision.HIGHEST)
        + prefix_shifts
    )
    return trajectory


def solution(mesh):
    placed = (P(("groups", "seq"), None), P(("groups", "seq"), None), P("groups"), P(), P(), P())
    return jax.shard_map(
        per_device,
        mesh=mesh,
        in_specs=placed,
        out_specs=P(("groups", "seq"), None),
        check_vma=False,
    )
```

profile of v0, /device:TPU:0, one launch (start us, length us, event | category | flops | bytes accessed | tf_op | source)
XLA Modules:
  0.0 212.2 jit_solution(2211586808047167283)
XLA Ops:
  6.5 0.7 slice.320
  7.3 2.3 %collective-permute-start = (f32[1,128]{1,0:T(1,128)S(1)}, f32[1,128]{1,0:T(1,128)S(1)}, u32[]{:S(2)}, u32[]{:S(2)}) collective-permute-start(f32[1,128]{1,0:T(1,128)S(1)} %slice.320), channel_id=1, source_target_pairs={{0,1},{1,2},{2,3},{3,4},{4,5},{5,6},{6,7},{7,8},{8,9},{9,10},{10,1... | collective-permute-start | bytes 1544 | tf_op jit(solution)/shard_map/ppermute | solution.py:10
  9.6 0.9 fusion.118
  10.6 1.0 convolution_add_fusion
  12.3 1.2 fusion.90
  13.5 0.8 add_subtract_fusion
  14.3 0.8 multiply_multiply_fusion
  15.1 1.0 multiply_add_fusion
  16.1 2.2 %fusion.2 = f32[32,128,128]{2,1,0:T(8,128)S(1)} fusion(f32[64,128,128]{2,1,0:T(8,128)S(1)} %multiply_add_fusion), kind=kOutput, calls=%fused_computation.4 | convolution fusion | flops 805306368 | bytes 6291456 | tf_op jit(solution)/shard_map/...ki,...ij->...kj/dot_general | solution.py:30
  18.4 1.9 fusion.4
  20.3 1.1 fusion.14
  21.4 1.0 fusion.16
  23.0 1.5 fusion.25
  25.1 2.1 %fusion.43 = f32[4,128,128]{2,1,0:T(8,128)} fusion(f32[8,128,128]{2,1,0:T(8,128)} %fusion.25), kind=kOutput, calls=%fused_computation.60 | convolution fusion | flops 100663296 | bytes 786432 | tf_op jit(solution)/shard_map/...ki,...ij->...kj/dot_general | solution.py:30
  27.2 1.3 fusion.48
  31.3 1.2 fusion.61
  32.5 1.1 fusion.66
  35.0 1.5 convolution_add_fusion.3
  36.6 1.7 pad.147
  38.3 1.2 pad_maximum_fusion.16
  39.5 1.7 pad.146
  42.9 1.9 pad.149
  44.8 1.3 slice.397
  46.1 1.2 fusion.55
  48.0 1.2 pad_maximum_fusion.14
  49.1 1.8 pad.148
  52.8 1.9 pad.151
  54.9 1.7 convolution_bitcast_fusion.2
  56.6 1.5 slice.431
  58.1 1.5 pad.127
  59.6 0.9 pad_maximum_fusion.6
  60.5 1.4 pad.126
  61.9 1.1 add.260
  63.0 0.7 copy-done.7
  63.7 1.9 fusion.57
  65.6 3.7 %pad.129 = f32[8,128,128]{2,1,0:T(8,128)} pad(f32[4,128,128]{2,1,0:T(8,128)} %copy-done.7, f32[]{:T(128)} %constant.20.clone.1), padding=1_0_1x0_0_0x0_0_0 | pad | bytes 786436 | tf_op jit(solution)/shard_map/pad | solution.py:61
  69.4 1.7 pad_maximum_fusion.4
  71.0 3.7 %pad.128 = f32[8,128,128]{2,1,0:T(8,128)} pad(f32[4,128,128]{2,1,0:T(8,128)} %pad_maximum_fusion.4, f32[]{:T(128)} %constant.20.clone.1), padding=0_1_1x0_0_0x0_0_0 | pad | bytes 786436 | tf_op jit(solution)/shard_map/pad | solution.py:61
  74.8 1.3 add.261
  76.0 0.8 copy-done.5
  76.8 1.4 fusion.39
  78.2 5.7 %pad.131 = f32[16,128,128]{2,1,0:T(8,128)} pad(f32[8,128,128]{2,1,0:T(8,128)} %copy-done.5, f32[]{:T(128)} %constant.20.clone.1), padding=1_0_1x0_0_0x0_0_0 | pad | bytes 1572868 | tf_op jit(solution)/shard_map/pad | solution.py:61
  84.0 1.9 pad_maximum_fusion.2
  85.8 5.7 %pad.130 = f32[16,128,128]{2,1,0:T(8,128)} pad(f32[8,128,128]{2,1,0:T(8,128)} %pad_maximum_fusion.2, f32[]{:T(128)} %constant.20.clone.1), padding=0_1_1x0_0_0x0_0_0 | pad | bytes 1572868 | tf_op jit(solution)/shard_map/pad | solution.py:61
  91.6 1.7 add.262
  93.2 0.9 copy-done.6
  94.2 2.2 %fusion.21 = f32[15,128,128]{2,1,0:T(8,128)} fusion(f32[16,128,128]{2,1,0:T(8,128)S(1)} %add.262, f32[32,128,128]{2,1,0:T(8,128)S(1)} %fusion.2), kind=kOutput, calls=%fused_computation.34 | convolution fusion | flops 377487360 | bytes 3014656 | tf_op jit(solution)/shard_map/...ki,...ij->...kj/dot_general | solution.py:30
  96.3 10.2 %pad.133 = f32[32,128,128]{2,1,0:T(8,128)} pad(f32[16,128,128]{2,1,0:T(8,128)} %copy-done.6, f32[]{:T(128)} %constant.20.clone.1), padding=1_0_1x0_0_0x0_0_0 | pad | bytes 3145732 | tf_op jit(solution)/shard_map/pad | solution.py:61
  106.5 1.3 pad_maximum_fusion.1
  107.8 6.4 %pad.132 = f32[32,128,128]{2,1,0:T(8,128)} pad(f32[16,128,128]{2,1,0:T(8,128)S(1)} %pad_maximum_fusion.1, f32[]{:T(128)} %constant.20.clone.1), padding=0_1_1x0_0_0x0_0_0 | pad | bytes 3145732 | tf_op jit(solution)/shard_map/pad | solution.py:61
  114.2 2.6 %add.263 = f32[32,128,128]{2,1,0:T(8,128)S(1)} add(f32[32,128,128]{2,1,0:T(8,128)} %pad.132, f32[32,128,128]{2,1,0:T(8,128)} %pad.133) | non-fusion elementwise | flops 524288 | bytes 6291456 | tf_op jit(solution)/shard_map/add | solution.py:61
  116.9 0.8 copy-done.2
  117.7 3.5 %fusion.9 = f32[31,128,128]{2,1,0:T(8,128)} fusion(f32[32,128,128]{2,1,0:T(8,128)S(1)} %add.263, f32[64,128,128]{2,1,0:T(8,128)S(1)} %copy-done.2), kind=kOutput, calls=%fused_computation.11 | convolution fusion | flops 780140544 | bytes 6160384 | tf_op jit(solution)/shard_map/...ki,...ij->...kj/dot_general | solution.py:30
  121.2 12.0 %pad.135 = f32[64,128,128]{2,1,0:T(8,128)} pad(f32[32,128,128]{2,1,0:T(8,128)S(1)} %add.263, f32[]{:T(128)} %constant.20.clone.1), padding=1_0_1x0_0_0x0_0_0 | pad | bytes 6291460 | tf_op jit(solution)/shard_map/pad | solution.py:61
  133.8 1.7 pad_maximum_fusion
  135.5 12.0 %pad.134 = f32[64,128,128]{2,1,0:T(8,128)} pad(f32[32,128,128]{2,1,0:T(8,128)S(1)} %pad_maximum_fusion, f32[]{:T(128)} %constant.20.clone.1), padding=0_1_1x0_0_0x0_0_0 | pad | bytes 6291460 | tf_op jit(solution)/shard_map/pad | solution.py:61
  147.6 1.5 slice_add_fusion
  149.2 2.1 fusion.19
  151.4 3.4 %fusion.7 = f32[31,1,128]{2,1,0:T(1,128)S(1)} fusion(f32[64,128,128]{2,1,0:T(8,128)} %copy-done.1, f32[31,128,1]{1,0,2:T(8,128)S(1)} %add_bitcast_fusion), kind=kOutput, calls=%fused_computation.9 | convolution fusion | flops 6094848 | bytes 2063360 | tf_op jit(solution)/shard_map/...i,...ij->...j/dot_general | solution.py:32
  154.8 23.5 %all-gather = f32[16,1,128]{2,1,0:T(1,128)S(1)} all-gather(f32[1,1,128]{2,1,0:T(1,128)S(1)} %add_bitcast_fusion.2), channel_id=1, replica_groups=mesh['groups'=2,'seq'=16] {'seq'}, dimensions={0}, use_global_device_ids=true | all-gather | bytes 8704 | tf_op jit(solution)/shard_map/all_gather | solution.py:66
  178.3 12.1 %all-gather.3.cloned.1.call-done = f32[16,128,128]{2,1,0:T(8,128)} async-done(((f32[1,128,128]{2,1,0:T(8,128)}), f32[16,128,128]{2,1,0:T(8,128)}) %all-gather.3.cloned.1.call-update) | async-done | bytes 1048592 | tf_op jit(solution)/shard_map/all_gather | solution.py:65
  190.4 1.7 fusion.27
  192.1 1.8 fusion.23
  199.1 5.7 %fusion = f32[1,64,128]{2,0,1:T(1,128)S(1)} fusion(f32[128,1,1]{0,1,2:T(1,128)S(1)} %fusion.13, f32[64,128,128]{2,1,0:T(8,128)} %pad.134, f32[64,128,128]{2,1,0:T(8,128)} %pad.135), kind=kOutput, calls=%fused_computation | convolution fusion | flops 13631488 | bytes 8421888 | tf_op jit(solution)/shard_map/k,tkj->tj/dot_general | solution.py:80
  (160 shorter events, 16.8 us)
Async XLA Ops:
  6.5 4.0 %copy-start = (f32[128,384]{1,0:T(8,128)S(1)}, f32[128,384]{1,0:T(8,128)}, u32[]{:S(2)}) copy-start(f32[128,384]{1,0:T(8,128)} %param.9) | copy-start | bytes 589828
  6.5 183.9 %all-gather.3.cloned.1.call-start = ((), (), s32[]{:S(2)}) async-start(), calls=%async_computation | async-start | bytes 1114112 | tf_op jit(solution)/shard_map/all_gather | solution.py:65
  7.3 4.3 %collective-permute-start = (f32[1,128]{1,0:T(1,128)S(1)}, f32[1,128]{1,0:T(1,128)S(1)}, u32[]{:S(2)}, u32[]{:S(2)}) collective-permute-start(f32[1,128]{1,0:T(1,128)S(1)} %slice.320), channel_id=1, source_target_pairs={{0,1},{1,2},{2,3},{3,4},{4,5},{5,6},{6,7},{7,8},{8,9},{9,10},{10,1... | collective-permute-start | bytes 1544 | tf_op jit(solution)/shard_map/ppermute | solution.py:10
  14.3 0.8 copy-start.8
  16.1 4.1 %copy-start.1 = (f32[64,128,128]{2,1,0:T(8,128)}, f32[64,128,128]{2,1,0:T(8,128)S(1)}, u32[]{:S(2)}) copy-start(f32[64,128,128]{2,1,0:T(8,128)S(1)} %multiply_add_fusion) | copy-start | bytes 12582916
  18.4 74.9 %copy-start.3 = (f32[32,128,128]{2,1,0:T(8,128)}, f32[32,128,128]{2,1,0:T(8,128)S(1)}, u32[]{:S(2)}) copy-start(f32[32,128,128]{2,1,0:T(8,128)S(1)} %fusion.2) | copy-start | bytes 6291460
  22.4 0.6 copy-start.11
  24.5 44.9 %slice-start.2 = ((f32[8,128,128]{2,1,0:T(8,128)}), f32[1,128,128]{2,1,0:T(8,128)S(1)}, s32[]{:S(2)}) async-start(f32[8,128,128]{2,1,0:T(8,128)} %fusion.25), calls=%async_computation.3 | async-start | bytes 131072 | tf_op jit(solution)/shard_map/slice | solution.py:61
  28.5 2.3 %copy-start.13 = (f32[4,128]{1,0:T(4,128)}, f32[4,128]{1,0:T(4,128)S(1)}, u32[]{:S(2)}) copy-start(f32[4,128]{1,0:T(4,128)S(1)} %add.276) | copy-start | bytes 6148
  34.5 0.5 copy-start.17
  41.8 0.6 copy-start.14
  51.6 0.6 copy-start.12
  63.0 0.7 copy-start.7
  76.0 0.8 copy-start.5
  93.2 1.0 copy-start.6
  114.2 3.4 %copy-start.2 = (f32[64,128,128]{2,1,0:T(8,128)S(1)}, f32[64,128,128]{2,1,0:T(8,128)}, u32[]{:S(2)}) copy-start(f32[64,128,128]{2,1,0:T(8,128)} %copy-done.1) | copy-start | bytes 12582916
  121.2 12.1 %copy-start.16 = (f32[7,128,1]{1,0,2:T(8,128)S(1)}, f32[7,128,1]{1,0,2:T(8,128)}, u32[]{:S(2)}) copy-start(f32[7,128,1]{1,0,2:T(8,128)} %slice_bitcast_fusion.13) | copy-start | bytes 10756
  121.2 12.5 %copy-start.15 = (f32[7,128]{1,0:T(8,128)S(1)}, f32[7,128]{1,0:T(8,128)}, u32[]{:S(2)}) copy-start(f32[7,128]{1,0:T(8,128)} %slice.397) | copy-start | bytes 10756
  121.2 12.5 %slice-start.3 = ((f32[16,128]{1,0:T(8,128)}), f32[1,128]{1,0:T(1,128)S(1)}, s32[]{:S(2)}) async-start(f32[16,128]{1,0:T(8,128)} %copy-done.11), calls=%async_computation.4 | async-start | bytes 1024 | tf_op jit(solution)/shard_map/slice | solution.py:61
  121.2 12.6 %slice-start = ((f32[64,128,128]{2,1,0:T(8,128)}), f32[1,128,128]{2,1,0:T(8,128)S(1)}, s32[]{:S(2)}) async-start(f32[64,128,128]{2,1,0:T(8,128)} %copy-done.1), calls=%async_computation.1 | async-start | bytes 131072 | tf_op jit(solution)/shard_map/slice | solution.py:61
  135.5 13.6 %copy-start.10 = (f32[16,128]{1,0:T(8,128)S(1)}, f32[16,128]{1,0:T(8,128)}, u32[]{:S(2)}) copy-start(f32[16,128]{1,0:T(8,128)} %pad.151) | copy-start | bytes 24580
  135.5 13.6 %copy-start.9 = (f32[64,128]{1,0:T(8,128)S(1)}, f32[64,128]{1,0:T(8,128)}, u32[]{:S(2)}) copy-start(f32[64,128]{1,0:T(8,128)} %copy-done.8) | copy-start | bytes 98308
  190.4 6.9 %copy-start.4 = (f32[16,128,128]{2,1,0:T(8,128)S(1)}, f32[16,128,128]{2,1,0:T(8,128)}, u32[]{:S(2)}) copy-start(f32[16,128,128]{2,1,0:T(8,128)} %all-gather.3.cloned.1.call-done) | copy-start | bytes 3145732
  196.8 1.9 slice-start.1
  197.8 1.1 copy-start.18
Sparse Core Ops, SparseCore 0:
  149.2 41.1 all-gather.2
where the time goes:
time: 215 us; the launch traced here: 212 us
  local copies, waits for them, and re-layouts  86.6 us (40%)
  matrix products  48.7 us (23%)
  other arithmetic  24.8 us (12%)
  blocking collectives  23.5 us (11%)
  between operations  14.2 us (7%)
  waiting for transfers between devices  12.1 us (6%)
  starting transfers between devices  2.35 us (1%)
    pad x20, local copies, waits for them, and re-layouts, per_device(): lax.associative_scan(compose, (step_maps, offset))  71.6 us
    all_gather x1, blocking collectives, per_device(): lax.all_gather(total_shift[None], 'seq', axis=0, tiled=True)  23.5 us
    dot_general x18, matrix products, compose(): jnp.einsum('...ki,...ij->...kj', map_early, map_late, precision=lax.Preci...  22.9 us
    dot_general x18, matrix products, compose(): jnp.einsum('...i,...ij->...j', shift_early, map_late, precision=lax.Preci...  17.8 us
    all_gather x1, waiting for transfers between devices, per_device(): lax.all_gather(total_map[None], 'seq', axis=0, tiled=True)  12.1 us
    concatenate x10, other arithmetic, per_device(): lax.associative_scan(compose, (step_maps, offset))  9.78 us
    add x11, other arithmetic, per_device(): lax.associative_scan(compose, (step_maps, offset))  9.44 us
    slice x31, local copies, waits for them, and re-layouts, per_device(): lax.associative_scan(compose, (step_maps, offset))  6.86 us
  transfers between devices with their start and end apart: 2, of which 1 were waited for; matrix products, arithmetic and copies ran while one was open for 4% of the time, Pallas kernels for 0%

commit v1 on v0

v1 whole, which is shorter than its diff:
```python
import functools
import math

import jax
import jax.numpy as jnp
from jax import lax
from jax.experimental import pallas as pl
from jax.experimental.pallas import tpu as pltpu
from jax.sharding import PartitionSpec as P

TAIL = 16
SENT = 8
BATCH = 4


def split(value):
    high = value.astype(jnp.bfloat16)
    low = (value - high.astype(jnp.float32)).astype(jnp.bfloat16)
    return high, low


def product(left, right):
    lh, ll = split(left)
    rh, rl = split(right)
    parts = jnp.concatenate([rh, rl], axis=1)
    both = jnp.dot(
        jnp.concatenate([lh, ll], axis=1),
        jnp.concatenate([parts, parts], axis=0),
        preferred_element_type=jnp.float32,
    )
    width = right.shape[1]
    return both[:, :width] + both[:, width:]


def compose(early, late):
    width = late.shape[1]
    moved = product(early, late[:width])
    return moved[:width], moved[width:] + late[width:]


def column(row):
    width = row.shape[1]
    return jnp.broadcast_to(row, (width, width)).T


def kernel(
    count, group,
    inputs, guesses, initial, w_input, w_hidden, biases, out,
    maps, prev, upd, cz_, cn_, cr_, off, arrived, incl, excl, state, state_next,
    row_send, row_recv, map_send, map_recv, state_send, state_recv,
):
    steps, width = guesses.shape
    levels = int(math.log2(group))
    me = lax.axis_index("seq")
    place = lax.rem(me, group)
    first_group = me < group
    last_group = me >= count - group
    leader = place == group - 1
    forwards = jnp.logical_and(leader, jnp.logical_not(last_group))

    def upper(level):
        return lax.rem(lax.div(me, 2**level), 2) == 1

    def sends(level):
        return lax.rem(me, 2 ** (level + 1)) == 2**level - 1

    def row_copy():
        return pltpu.make_async_remote_copy(
            src_ref=guesses.at[pl.ds(steps - 8, 8)], dst_ref=prev.at[pl.ds(0, 8)],
            send_sem=row_send, recv_sem=row_recv, device_id={"seq": me + 1})

    def map_copy(level, which):
        src = maps.at[steps - 1] if level == 0 else incl.at[level - 1]
        return pltpu.make_async_remote_copy(
            src_ref=src.at[pl.ds(0, width + SENT)],
            dst_ref=arrived.at[level, pl.ds(0, width + SENT)],
            send_sem=map_send.at[2**level - 1 + which], recv_sem=map_recv.at[level],
            device_id={"seq": me + 1 + which})

    def state_copy(which):
        return pltpu.make_async_remote_copy(
            src_ref=state_next, dst_ref=state,
            send_sem=state_send.at[which], recv_sem=state_recv,
            device_id={"seq": me + 1 + which})

    barrier = pltpu.get_barrier_semaphore()

    @pl.when(me > 0)
    def _():
        pl.semaphore_signal(barrier, 1, device_id={"seq": me - 1})

    for level in range(levels):
        @pl.when(upper(level))
        def _():
            source = lax.div(me, 2**level) * 2**level - 1
            pl.semaphore_signal(barrier, 1, device_id={"seq": source})

    @pl.when(jnp.logical_not(first_group))
    def _():
        pl.semaphore_signal(barrier, 1, device_id={"seq": lax.div(me, group) * group - 1})

    copies = 1 + group * forwards.astype(jnp.int32)
    for level in range(levels):
        copies += 2**level * sends(level).astype(jnp.int32)

    @pl.when(me < count - 1)
    def _():
        pl.semaphore_wait(barrier, copies)

    @pl.when(me < count - 1)
    def _():
        row_copy().start()

    prev[pl.ds(8, steps), :] = guesses[...]

    @pl.when(me == 0)
    def _():
        prev[pl.ds(7, 1), :] = initial[...][None, :]

    pre = product(inputs[...], w_input[...]) + biases[...][None, :]

    @pl.when(me > 0)
    def _():
        row_copy().wait_recv()

    previous = prev[pl.ds(7, steps), :]
    rec = product(previous, w_hidden[...])
    pz, pr, pn = (pre[:, :width], pre[:, width : 2 * width], pre[:, 2 * width :])
    cz, cr, cn = (rec[:, :width], rec[:, width : 2 * width], rec[:, 2 * width :])
    update = jax.nn.sigmoid(pz + cz)
    reset = jax.nn.sigmoid(pr + cr)
    cand = jnp.tanh(pn + reset * cn)
    value = (1.0 - update) * cand + update * previous
    coef_update = (previous - cand) * update * (1.0 - update)
    coef_cand = (1.0 - update) * (1.0 - cand * cand) * reset
    coef_reset = (1.0 - update) * (1.0 - cand * cand) * cn * reset * (1.0 - reset)
    upd[...] = update
    cz_[...] = coef_update
    cn_[...] = coef_cand
    cr_[...] = coef_reset
    off[...] = value - (update * previous + coef_update * cz + coef_cand * cn + coef_reset * cr)

    rows = lax.broadcasted_iota(jnp.int32, (width, width), 0)
    cols = lax.broadcasted_iota(jnp.int32, (width, width), 1)
    top = lax.broadcasted_iota(jnp.int32, (TAIL, width), 0) == 0

    def step_map(t, _):
        one = pl.ds(t, 1)
        maps[t, :width, :] = (
            jnp.where(rows == cols, upd[one, :], 0.0)
            + cz_[one, :] * w_hidden[:, :width]
            + cr_[one, :] * w_hidden[:, width : 2 * width]
            + cn_[one, :] * w_hidden[:, 2 * width :]
        )
        maps[t, width:, :] = jnp.where(top, off[one, :], 0.0)
        return 0

    lax.fori_loop(0, steps, step_map, 0)

    def sweep(first, stride, distance, number):
        batch = min(BATCH, number)

        def some(start, size):
            where = [start + stride * j for j in range(size)]
            news = [compose(maps[i - distance], maps[i]) for i in where]
            for i, (new_map, new_tail) in zip(where, news):
                maps[i, :width, :] = new_map
                maps[i, width:, :] = new_tail

        def body(j, _):
            some(first + j * (stride * batch), batch)
            return 0

        whole = number // batch
        if whole > 1:
            lax.fori_loop(0, whole, body, 0)
        else:
            some(first, batch)
        if number % batch:
            some(first + whole * batch * stride, number % batch)

    distance = 1
    while distance < steps:
        sweep(2 * distance - 1, 2 * distance, distance, steps // (2 * distance))
        distance *= 2

    down = []
    distance = steps // 4
    while distance >= 1:
        down.append((3 * distance - 1, 2 * distance, distance, steps // (2 * distance) - 1))
        distance //= 2

    eye = jnp.where(rows == cols, 1.0, 0.0)
    excl[:width, :] = eye
    excl[width:, :] = jnp.zeros((TAIL, width), jnp.float32)
    share = {0: down[:-2], 1: down[-2:-1]}
    for level in range(levels):
        @pl.when(sends(level))
        def _():
            for which in range(2**level):
                map_copy(level, 2**level - 1 - which).start()

        for item in share.get(level, ()):
            sweep(*item)

        held = maps.at[steps - 1] if level == 0 else incl.at[level - 1]

        @pl.when(upper(level))
        def _():
            map_copy(level, 0).wait_recv()
            arrived[level, pl.ds(width + SENT, TAIL - SENT), :] = jnp.zeros(
                (TAIL - SENT, width), jnp.float32)
            early = arrived[level]
            new_map, new_tail = compose(early, held[...])
            incl[level, :width, :] = new_map
            incl[level, width:, :] = new_tail
            new_map, new_tail = compose(early, excl[...])
            excl[:width, :] = new_map
            excl[width:, :] = new_tail

        @pl.when(jnp.logical_not(upper(level)))
        def _():
            incl[level] = held[...]

    @pl.when(first_group)
    def _():
        state[...] = jnp.broadcast_to(initial[...][None, :], state.shape)

    @pl.when(forwards)
    def _():
        @pl.when(jnp.logical_not(first_group))
        def _():
            state_copy(0).wait_recv()
        whole = incl.at[levels - 1]
        moved = jnp.sum(column(state[0:1, :]) * whole[:width, :], axis=0, keepdims=True)
        state_next[...] = jnp.broadcast_to(moved + whole[width : width + 1, :], state_next.shape)
        for which in range(group):
            state_copy(group - 1 - which).start()

    for item in down[-1:]:
        sweep(*item)

    @pl.when(jnp.logical_not(jnp.logical_or(forwards, first_group)))
    def _():
        state_copy(0).wait_recv()

    entry = jnp.sum(column(state[0:1, :]) * excl[:width, :], axis=0, keepdims=True)
    across = column(entry + excl[width : width + 1, :])

    def finish(j, _):
        lines = []
        for k in range(8):
            t = j * 8 + k
            line = jnp.sum(across * maps[t, :width, :], axis=0, keepdims=True)
            lines.append(line + maps[t, width : width + 1, :])
        out[pl.ds(pl.multiple_of(j * 8, 8), 8), :] = jnp.concatenate(lines, axis=0)
        return 0

    lax.fori_loop(0, steps // 8, finish, 0)

    @pl.when(me < count - 1)
    def _():
        row_copy().wait_send()

    for level in range(levels):
        @pl.when(sends(level))
        def _():
            for which in range(2**level):
                map_copy(level, which).wait_send()

    @pl.when(forwards)
    def _():
        for which in range(group):
            state_copy(which).wait_send()


def solution(mesh):
    count = mesh.shape["seq"]
    group = 4

    def per_device(inputs, guesses, initial, w_input, w_hidden, biases):
        steps, width = guesses.shape
        levels = int(math.log2(group))
        full = width + TAIL
        line = pltpu.VMEM((steps, width), jnp.float32)
        return pl.pallas_call(
            functools.partial(kernel, count, group),
            out_shape=jax.ShapeDtypeStruct((steps, width), jnp.float32),
            in_specs=[pl.BlockSpec(memory_space=pltpu.VMEM)] * 6,
            out_specs=pl.BlockSpec(memory_space=pltpu.VMEM),
            scratch_shapes=[
                pltpu.VMEM((steps, full, width), jnp.float32),
                pltpu.VMEM((steps + 8, width), jnp.float32),
                line, line, line, line, line,
                pltpu.VMEM((levels, full, width), jnp.float32),
                pltpu.VMEM((levels, full, width), jnp.float32),
                pltpu.VMEM((full, width), jnp.float32),
                pltpu.VMEM((8, width), jnp.float32),
                pltpu.VMEM((8, width), jnp.float32),
                pltpu.SemaphoreType.DMA,
                pltpu.SemaphoreType.DMA,
                pltpu.SemaphoreType.DMA((group - 1,)),
                pltpu.SemaphoreType.DMA((levels,)),
                pltpu.SemaphoreType.DMA((group,)),
                pltpu.SemaphoreType.DMA,
            ],
            compiler_params=pltpu.CompilerParams(
                collective_id=0, has_side_effects=True, vmem_limit_bytes=32 * 2**20),
        )(inputs, guesses, initial, w_input, w_hidden, biases)

    placed = (P(("groups", "seq"), None), P(("groups", "seq"), None), P("groups"), P(), P(), P())
    return jax.shard_map(
        per_device,
        mesh=mesh,
        in_specs=placed,
        out_specs=P(("groups", "seq"), None),
        check_vma=False,
    )
```

time: 215 us -> 23.6 us (0.11)
  the two profiles are of different devices: /device:TPU:0 before, /device:TPU:28 now
where the time goes in v1:
time: 23.6 us; the launch traced here: 23.3 us
  Pallas kernels  17.9 us (76%)
  local copies, waits for them, and re-layouts  5.32 us (23%)
    pallas_call x1, Pallas kernels, per_device(): pl.pallas_call(functools.partial(kernel, count, group), out_shape=jax.Sha...  17.9 us
    unnamed x13, local copies, waits for them, and re-layouts  5.32 us

profile of v1, /device:TPU:28, one launch (start us, length us, event | category | flops | bytes accessed | tf_op | source)
XLA Modules:
  0.0 23.3 jit_solution(5766604253781148483)
XLA Ops:
  0.0 0.0 copy-start
  0.0 0.9 %copy-done = f32[128,384]{1,0:T(8,128)S(1)} copy-done((f32[128,384]{1,0:T(8,128)S(1)}, f32[128,384]{1,0:T(8,128)}, u32[]{:S(2)}) %copy-start) | copy-done | bytes 196632
  0.9 0.0 copy-start.1
  0.9 0.9 %copy-done.1 = f32[128,384]{1,0:T(8,128)S(1)} copy-done((f32[128,384]{1,0:T(8,128)S(1)}, f32[128,384]{1,0:T(8,128)}, u32[]{:S(2)}) %copy-start.1) | copy-done | bytes 196632
  1.9 0.0 copy-start.2
  1.9 0.8 %copy-done.2 = f32[64,128]{1,0:T(8,128)S(1)} copy-done((f32[64,128]{1,0:T(8,128)S(1)}, f32[64,128]{1,0:T(8,128)}, u32[]{:S(2)}) %copy-start.2) | copy-done | bytes 32792
  2.6 0.0 copy-start.3
  2.6 0.8 %copy-done.3 = f32[64,128]{1,0:T(8,128)S(1)} copy-done((f32[64,128]{1,0:T(8,128)S(1)}, f32[64,128]{1,0:T(8,128)}, u32[]{:S(2)}) %copy-start.3) | copy-done | bytes 32792
  3.4 0.0 copy-start.4
  3.4 0.7 %copy-done.4 = f32[384]{0:T(512)S(1)} copy-done((f32[384]{0:T(512)S(1)}, f32[384]{0:T(512)}, u32[]{:S(2)}) %copy-start.4) | copy-done | bytes 1560
  4.1 0.0 copy-start.5
  4.1 0.7 %copy-done.5 = f32[128]{0:T(128)S(1)} copy-done((f32[128]{0:T(128)S(1)}, f32[128]{0:T(128)}, u32[]{:S(2)}) %copy-start.5) | copy-done | bytes 536
  4.7 17.9 %shard_map.64 = f32[64,128]{1,0:T(8,128)S(1)} custom-call(f32[64,128]{1,0:T(8,128)S(1)} %copy-done.2, f32[64,128]{1,0:T(8,128)S(1)} %copy-done.3, f32[128]{0:T(128)S(1)} %copy-done.5, f32[128,384]{1,0:T(8,128)S(1)} %copy-done, f32[128,384]{1,0:T(8,128)S(1)} %copy-done.1, f32[384]{0:T(512)S(1)} %copy-done.4), custom_call_target="tpu_custom_call" | custom-call | tf_op jit(solution)/shard_map/pallas_call | solution.py:286
  22.6 0.6 %copy.8 = f32[64,128]{1,0:T(8,128)} copy(f32[64,128]{1,0:T(8,128)S(1)} %shard_map.64) | data formatting | bytes 65536
Async XLA Ops:
  0.0 0.9 %copy-start = (f32[128,384]{1,0:T(8,128)S(1)}, f32[128,384]{1,0:T(8,128)}, u32[]{:S(2)}) copy-start(f32[128,384]{1,0:T(8,128)} %w_input.1) | copy-start | bytes 589828
  0.9 0.9 %copy-start.1 = (f32[128,384]{1,0:T(8,128)S(1)}, f32[128,384]{1,0:T(8,128)}, u32[]{:S(2)}) copy-start(f32[128,384]{1,0:T(8,128)} %w_hidden.1) | copy-start | bytes 589828
  1.9 0.8 %copy-start.2 = (f32[64,128]{1,0:T(8,128)S(1)}, f32[64,128]{1,0:T(8,128)}, u32[]{:S(2)}) copy-start(f32[64,128]{1,0:T(8,128)} %inputs.1) | copy-start | bytes 98308
  2.6 0.8 %copy-start.3 = (f32[64,128]{1,0:T(8,128)S(1)}, f32[64,128]{1,0:T(8,128)}, u32[]{:S(2)}) copy-start(f32[64,128]{1,0:T(8,128)} %guesses.1) | copy-start | bytes 98308
  3.4 0.7 %copy-start.4 = (f32[384]{0:T(512)S(1)}, f32[384]{0:T(512)}, u32[]{:S(2)}) copy-start(f32[384]{0:T(512)} %biases.1) | copy-start | bytes 4612
  4.1 0.7 %copy-start.5 = (f32[128]{0:T(128)S(1)}, f32[128]{0:T(128)}, u32[]{:S(2)}) copy-start(f32[128]{0:T(128)} %initial.1) | copy-start | bytes 1540

commit v2 on v1

v2 whole, which is shorter than its diff:
```python
import functools
import math

import jax
import jax.numpy as jnp
from jax import lax
from jax.experimental import pallas as pl
from jax.experimental.pallas import tpu as pltpu
from jax.sharding import PartitionSpec as P

TAIL = 16
SENT = 8
BATCH = 4
PAIRS = 3


def split(value):
    high = value.astype(jnp.bfloat16)
    low = (value - high.astype(jnp.float32)).astype(jnp.bfloat16)
    return high, low


def product(left, right):
    lh, ll = split(left)
    rh, rl = split(right)
    parts = jnp.concatenate([rh, rl], axis=1)
    both = jnp.dot(
        jnp.concatenate([lh, ll], axis=1),
        jnp.concatenate([parts, parts], axis=0),
        preferred_element_type=jnp.float32,
    )
    width = right.shape[1]
    return both[:, :width] + both[:, width:]


def compose(early, late):
    width = late.shape[1]
    moved = product(early, late[:width])
    return moved[:width], moved[width:] + late[width:]


def column(row):
    width = row.shape[1]
    return jnp.broadcast_to(row, (width, width)).T


def gates(previous, pre, rec):
    width = previous.shape[1]
    pz, pr, pn = (pre[:, :width], pre[:, width : 2 * width], pre[:, 2 * width :])
    cz, cr, cn = (rec[:, :width], rec[:, width : 2 * width], rec[:, 2 * width :])
    update = jax.nn.sigmoid(pz + cz)
    reset = jax.nn.sigmoid(pr + cr)
    cand = jnp.tanh(pn + reset * cn)
    value = (1.0 - update) * cand + update * previous
    coef_update = (previous - cand) * update * (1.0 - update)
    coef_cand = (1.0 - update) * (1.0 - cand * cand) * reset
    coef_reset = (1.0 - update) * (1.0 - cand * cand) * cn * reset * (1.0 - reset)
    offset = value - (update * previous + coef_update * cz + coef_cand * cn + coef_reset * cr)
    return update, coef_update, coef_reset, coef_cand, offset


def kernel(
    count, group,
    inputs_hbm, guesses_hbm, initial_hbm, w_input_hbm, w_hidden_hbm, biases_hbm, out,
    inputs, initial, w_input, w_hidden, biases, packed,
    maps, prev, landed, pre_first, coefs, odd, arrived, incl, excl, state, state_next,
    load_sem, row_send, row_recv, map_send, map_recv, state_send, state_recv,
):
    steps, width = inputs.shape
    levels = int(math.log2(group))
    me = lax.axis_index("seq")
    place = lax.rem(me, group)
    first_group = me < group
    last_group = me >= count - group
    leader = place == group - 1
    forwards = jnp.logical_and(leader, jnp.logical_not(last_group))

    def upper(level):
        return lax.rem(lax.div(me, 2**level), 2) == 1

    def sends(level):
        return lax.rem(me, 2 ** (level + 1)) == 2**level - 1

    def row_copy():
        return pltpu.make_async_remote_copy(
            src_ref=prev.at[pl.ds(steps, 8)], dst_ref=landed,
            send_sem=row_send, recv_sem=row_recv, device_id={"seq": me + 1})

    def map_copy(level, which):
        src = maps.at[steps // 2 - 1] if level == 0 else incl.at[level - 1]
        return pltpu.make_async_remote_copy(
            src_ref=src.at[pl.ds(0, width + SENT)],
            dst_ref=arrived.at[level, pl.ds(0, width + SENT)],
            send_sem=map_send.at[2**level - 1 + which], recv_sem=map_recv.at[level],
            device_id={"seq": me + 1 + which})

    def state_copy(which):
        return pltpu.make_async_remote_copy(
            src_ref=state_next, dst_ref=state,
            send_sem=state_send.at[which], recv_sem=state_recv,
            device_id={"seq": me + 1 + which})

    loads = [
        pltpu.make_async_copy(src, dst, load_sem.at[k])
        for k, (src, dst) in enumerate([
            (w_hidden_hbm, w_hidden), (w_input_hbm, w_input),
            (guesses_hbm, prev.at[pl.ds(8, steps)]), (inputs_hbm, inputs),
            (initial_hbm, initial), (biases_hbm, biases)])
    ]
    for load in loads:
        load.start()

    barrier = pltpu.get_barrier_semaphore()

    @pl.when(me > 0)
    def _():
        pl.semaphore_signal(barrier, 1, device_id={"seq": me - 1})

    for level in range(levels):
        @pl.when(upper(level))
        def _():
            source = lax.div(me, 2**level) * 2**level - 1
            pl.semaphore_signal(barrier, 1, device_id={"seq": source})

    @pl.when(jnp.logical_not(first_group))
    def _():
        pl.semaphore_signal(barrier, 1, device_id={"seq": lax.div(me, group) * group - 1})

    for load in loads:
        load.wait()

    prev[pl.ds(0, 8), :] = jnp.broadcast_to(initial[...][None, :], (8, width))
    high, low = split(w_hidden[...])
    for half in range(2):
        packed[half * width : (half + 1) * width, : 3 * width] = high
        packed[half * width : (half + 1) * width, 3 * width :] = low

    def recurrent(rows):
        both = jnp.dot(
            jnp.concatenate(split(rows), axis=1), packed[...],
            preferred_element_type=jnp.float32)
        return both[:, : 3 * width] + both[:, 3 * width :]

    pre = product(inputs[...], w_input[...]) + biases[...][None, :]
    pre_first[...] = pre[:16]
    previous = prev[pl.ds(7, steps), :]
    for k, part in enumerate(gates(previous, pre, recurrent(previous))):
        coefs[k] = part

    copies = 1 + group * forwards.astype(jnp.int32)
    for level in range(levels):
        copies += 2**level * sends(level).astype(jnp.int32)

    @pl.when(me < count - 1)
    def _():
        pl.semaphore_wait(barrier, copies)
        row_copy().start()

    rows = lax.broadcasted_iota(jnp.int32, (width, width), 0)
    cols = lax.broadcasted_iota(jnp.int32, (width, width), 1)
    top = lax.broadcasted_iota(jnp.int32, (TAIL, width), 0) == 0

    def step_map(t):
        one = pl.ds(t, 1)
        upd, cz, cr, cn, off = [coefs[k, one, :] for k in range(5)]
        body = (
            jnp.where(rows == cols, upd, 0.0)
            + cz * w_hidden[:, :width]
            + cr * w_hidden[:, width : 2 * width]
            + cn * w_hidden[:, 2 * width :]
        )
        return jnp.concatenate([body, jnp.where(top, off, 0.0)], axis=0)

    def store(ref, new):
        ref[:width, :] = new[0]
        ref[width:, :] = new[1]

    def pair(i):
        store(maps.at[i], compose(step_map(2 * i), step_map(2 * i + 1)))

    def pairs(start, size):
        news = [compose(step_map(2 * i), step_map(2 * i + 1))
                for i in [start + k for k in range(size)]]
        for k, new in enumerate(news):
            store(maps.at[start + k], new)

    def pairs_body(j, _):
        pairs(1 + PAIRS * j, PAIRS)
        return 0

    number = steps // 2
    whole = (number - 1) // PAIRS
    lax.fori_loop(0, whole, pairs_body, 0)

    @pl.when(me > 0)
    def _():
        row_copy().wait_recv()
        prev[pl.ds(7, 1), :] = landed[pl.ds(7, 1), :]
        fixed = prev[pl.ds(7, 16), :]
        for k, part in enumerate(gates(fixed, pre_first[...], recurrent(fixed))):
            coefs[k, :16, :] = part

    for i in [0] + list(range(1 + PAIRS * whole, number)):
        pair(i)

    def sweep(first, stride, distance, number):
        batch = min(BATCH, number)

        def some(start, size):
            where = [start + stride * j for j in range(size)]
            news = [compose(maps[i - distance], maps[i]) for i in where]
            for i, new in zip(where, news):
                store(maps.at[i], new)

        def body(j, _):
            some(first + j * (stride * batch), batch)
            return 0

        whole = number // batch
        if whole > 1:
            lax.fori_loop(0, whole, body, 0)
        else:
            some(first, batch)
        if number % batch:
            some(first + whole * batch * stride, number % batch)

    distance = 1
    while distance < number:
        sweep(2 * distance - 1, 2 * distance, distance, number // (2 * distance))
        distance *= 2

    down = []
    distance = number // 4
    while distance >= 1:
        down.append((3 * distance - 1, 2 * distance, distance, number // (2 * distance) - 1))
        distance //= 2

    excl[:width, :] = jnp.where(rows == cols, 1.0, 0.0)
    excl[width:, :] = jnp.zeros((TAIL, width), jnp.float32)
    share = {0: down[:-1]}
    for level in range(levels):
        @pl.when(sends(level))
        def _():
            for which in range(2**level):
                map_copy(level, 2**level - 1 - which).start()

        for item in share.get(level, ()):
            sweep(*item)

        held = maps.at[number - 1] if level == 0 else incl.at[level - 1]

        @pl.when(upper(level))
        def _():
            map_copy(level, 0).wait_recv()
            arrived[level, pl.ds(width + SENT, TAIL - SENT), :] = jnp.zeros(
                (TAIL - SENT, width), jnp.float32)
            early = arrived[level]
            store(incl.at[level], compose(early, held[...]))
            store(excl, compose(early, excl[...]))

        @pl.when(jnp.logical_not(upper(level)))
        def _():
            incl[level] = held[...]

    @pl.when(first_group)
    def _():
        state[...] = jnp.broadcast_to(initial[...][None, :], state.shape)

    @pl.when(forwards)
    def _():
        @pl.when(jnp.logical_not(first_group))
        def _():
            state_copy(0).wait_recv()
        whole = incl.at[levels - 1]
        moved = jnp.sum(column(state[0:1, :]) * whole[:width, :], axis=0, keepdims=True)
        state_next[...] = jnp.broadcast_to(
            moved + whole[width : width + 1, :], state_next.shape)
        for which in range(group):
            state_copy(group - 1 - which).start()

    for item in down[-1:]:
        sweep(*item)

    @pl.when(jnp.logical_not(jnp.logical_or(forwards, first_group)))
    def _():
        state_copy(0).wait_recv()

    entry = jnp.sum(column(state[0:1, :]) * excl[:width, :], axis=0, keepdims=True)
    entry = entry + excl[width : width + 1, :]
    across = column(entry)
    odd[0:8, :] = jnp.broadcast_to(entry, (8, width))

    def finish(j, _):
        lines = []
        for k in range(8):
            i = j * 8 + k
            line = jnp.sum(across * maps[i, :width, :], axis=0, keepdims=True)
            lines.append(line + maps[i, width : width + 1, :])
        odd[pl.ds(pl.multiple_of(8 + j * 8, 8), 8), :] = jnp.concatenate(lines, axis=0)
        return 0

    lax.fori_loop(0, number // 8, finish, 0)

    before = odd[pl.ds(7, number), :]
    rec = recurrent(before)
    even = pl.ds(0, number, 2)
    upd, cz, cr, cn, off = [coefs[k, even, :] for k in range(5)]
    out[even, :] = (
        upd * before + cz * rec[:, :width] + cr * rec[:, width : 2 * width]
        + cn * rec[:, 2 * width :] + off
    )
    out[pl.ds(1, number, 2), :] = odd[pl.ds(8, number), :]

    @pl.when(me < count - 1)
    def _():
        row_copy().wait_send()

    for level in range(levels):
        @pl.when(sends(level))
        def _():
            for which in range(2**level):
                map_copy(level, which).wait_send()

    @pl.when(forwards)
    def _():
        for which in range(group):
            state_copy(which).wait_send()


def solution(mesh):
    count = mesh.shape["seq"]
    group = 4

    def per_device(inputs, guesses, initial, w_input, w_hidden, biases):
        steps, width = guesses.shape
        levels = int(math.log2(group))
        full = width + TAIL
        line = pltpu.VMEM((steps, width), jnp.float32)
        return pl.pallas_call(
            functools.partial(kernel, count, group),
            out_shape=jax.ShapeDtypeStruct((steps, width), jnp.float32),
            in_specs=[pl.BlockSpec(memory_space=pl.ANY)] * 6,
            out_specs=pl.BlockSpec(memory_space=pltpu.VMEM),
            scratch_shapes=[
                pltpu.VMEM((steps, width), jnp.float32),
                pltpu.VMEM((width,), jnp.float32),
                pltpu.VMEM((width, 3 * width), jnp.float32),
                pltpu.VMEM((width, 3 * width), jnp.float32),
                pltpu.VMEM((3 * width,), jnp.float32),
                pltpu.VMEM((2 * width, 6 * width), jnp.bfloat16),
                pltpu.VMEM((steps // 2, full, width), jnp.float32),
                pltpu.VMEM((steps + 8, width), jnp.float32),
                pltpu.VMEM((8, width), jnp.float32),
                pltpu.VMEM((16, 3 * width), jnp.float32),
                pltpu.VMEM((5, steps, width), jnp.float32),
                pltpu.VMEM((steps // 2 + 8, width), jnp.float32),
                pltpu.VMEM((levels, full, width), jnp.float32),
                pltpu.VMEM((levels, full, width), jnp.float32),
                pltpu.VMEM((full, width), jnp.float32),
                pltpu.VMEM((8, width), jnp.float32),
                pltpu.VMEM((8, width), jnp.float32),
                pltpu.SemaphoreType.DMA((6,)),
                pltpu.SemaphoreType.DMA,
                pltpu.SemaphoreType.DMA,
                pltpu.SemaphoreType.DMA((group - 1,)),
                pltpu.SemaphoreType.DMA((levels,)),
                pltpu.SemaphoreType.DMA((group,)),
                pltpu.SemaphoreType.DMA,
            ],
            compiler_params=pltpu.CompilerParams(
                collective_id=0, has_side_effects=True, vmem_limit_bytes=56 * 2**20),
        )(inputs, guesses, initial, w_input, w_hidden, biases)

    placed = (P(("groups", "seq"), None), P(("groups", "seq"), None), P("groups"), P(), P(), P())
    return jax.shard_map(
        per_device,
        mesh=mesh,
        in_specs=placed,
        out_specs=P(("groups", "seq"), None),
        check_vma=False,
    )
```

time: 23.6 us -> 18.1 us (0.77)
  local copies, waits for them, and re-layouts: 5.32 us -> 1.38 us
  Pallas kernels: 17.9 us -> 16.5 us
    unnamed x13 -> x1, local copies, waits for them, and re-layouts: 5.32 us -> 1.38 us
    pallas_call x1, Pallas kernels: 17.9 us -> 16.5 us  [per_device(): pl.pallas_call(functools.partial(kernel, count, group), out_shape=jax.Sha...]
where the time goes in v2:
time: 18.1 us; the launch traced here: 17.9 us
  Pallas kernels  16.5 us (91%)
  local copies, waits for them, and re-layouts  1.38 us (8%)
    pallas_call x1, Pallas kernels, per_device(): pl.pallas_call(functools.partial(kernel, count, group), out_shape=jax.Sha...  16.5 us
    unnamed x1, local copies, waits for them, and re-layouts  1.38 us

profile of v2, /device:TPU:28, one launch (start us, length us, event | category | flops | bytes accessed | tf_op | source)
XLA Modules:
  0.0 17.9 jit_solution(7454319304008125347)
XLA Ops:
  0.0 16.5 %shard_map.64 = f32[64,128]{1,0:T(8,128)} custom-call(f32[64,128]{1,0:T(8,128)} %inputs_hbm.1, f32[64,128]{1,0:T(8,128)} %guesses_hbm.1, f32[128]{0:T(128)} %initial_hbm.1, f32[128,384]{1,0:T(8,128)} %w_input_hbm.1, f32[128,384]{1,0:T(8,128)} %w_hidden_hbm.1, f32[384]{0:T(512)} %biases_hbm.1), custom_call_target="tpu_custom_call" | custom-call | tf_op jit(solution)/shard_map/pallas_call | solution.py:339
  16.5 1.4 %copy.8 = f32[64,128]{1,0:T(8,128)} copy(f32[64,128]{1,0:T(8,128)} %shard_map.64) | data formatting | bytes 65536

commit v3 on v2

--- a/solution.py
+++ b/solution.py
@@ -57,6 +57,25 @@
     coef_reset = (1.0 - update) * (1.0 - cand * cand) * cn * reset * (1.0 - reset)
     offset = value - (update * previous + coef_update * cz + coef_cand * cn + coef_reset * cr)
     return update, coef_update, coef_reset, coef_cand, offset
+
+
+def store(ref, new):
+    width = new[0].shape[0]
+    ref[:width, :] = new[0]
+    ref[width:, :] = new[1]
+
+
+def exclude(level, me, excl, arrived, upper):
+    came = jnp.logical_and(upper(level), me >= 2 ** (level + 1))
+    below = lax.rem(me, 2**level) > 0
+
+    @pl.when(jnp.logical_and(came, below))
+    def _():
+        store(excl, compose(arrived[level], excl[...]))
+
+    @pl.when(jnp.logical_and(came, jnp.logical_not(below)))
+    def _():
+        excl[...] = arrived[level]
 
 
 def kernel(
@@ -171,10 +190,6 @@
         )
         return jnp.concatenate([body, jnp.where(top, off, 0.0)], axis=0)
 
-    def store(ref, new):
-        ref[:width, :] = new[0]
-        ref[width:, :] = new[1]
-
     def pair(i):
         store(maps.at[i], compose(step_map(2 * i), step_map(2 * i + 1)))
 
@@ -235,55 +250,77 @@
         down.append((3 * distance - 1, 2 * distance, distance, number // (2 * distance) - 1))
         distance //= 2
 
+    def held(level):
+        return maps.at[number - 1] if level == 0 else incl.at[level - 1]
+
+    def forward(ref, targets):
+        moved = jnp.sum(column(state[0:1, :]) * ref[:width, :], axis=0, keepdims=True)
+        state_next[...] = jnp.broadcast_to(
+            moved + ref[width : width + 1, :], state_next.shape)
+        for which in range(targets):
+            state_copy(targets - 1 - which).start()
+
+    def wait_state():
+        state_copy(0).wait_recv()
+
+    share = {0: down[:-2], 1: down[-2:-1]}
+
+    @pl.when(me == 0)
+    def _():
+        state[...] = jnp.broadcast_to(initial[...][None, :], state.shape)
+        forward(held(0), 1)
+
     excl[:width, :] = jnp.where(rows == cols, 1.0, 0.0)
     excl[width:, :] = jnp.zeros((TAIL, width), jnp.float32)
-    share = {0: down[:-1]}
     for level in range(levels):
-        @pl.when(sends(level))
+        @pl.when(jnp.logical_and(sends(level), me >= 2 ** (level + 1)))
         def _():
             for which in range(2**level):
                 map_copy(level, 2**level - 1 - which).start()
 
+        if level > 0:
+            @pl.when(me == 2**level - 1)
+            def _():
+                wait_state()
+                forward(held(level - 1), 2**level)
+
+            exclude(level - 1, me, excl, arrived, upper)
+
         for item in share.get(level, ()):
             sweep(*item)
 
-        held = maps.at[number - 1] if level == 0 else incl.at[level - 1]
-
-        @pl.when(upper(level))
+        @pl.when(jnp.logical_and(upper(level), me >= 2 ** (level + 1)))
         def _():
             map_copy(level, 0).wait_recv()
             arrived[level, pl.ds(width + SENT, TAIL - SENT), :] = jnp.zeros(
                 (TAIL - SENT, width), jnp.float32)
-            early = arrived[level]
-            store(incl.at[level], compose(early, held[...]))
-            store(excl, compose(early, excl[...]))
-
-        @pl.when(jnp.logical_not(upper(level)))
-        def _():
-            incl[level] = held[...]
-
-    @pl.when(first_group)
-    def _():
-        state[...] = jnp.broadcast_to(initial[...][None, :], state.shape)
-
-    @pl.when(forwards)
-    def _():
-        @pl.when(jnp.logical_not(first_group))
-        def _():
-            state_copy(0).wait_recv()
-        whole = incl.at[levels - 1]
-        moved = jnp.sum(column(state[0:1, :]) * whole[:width, :], axis=0, keepdims=True)
-        state_next[...] = jnp.broadcast_to(
-            moved + whole[width : width + 1, :], state_next.shape)
-        for which in range(group):
-            state_copy(group - 1 - which).start()
+
+            @pl.when(lax.rem(me, 2 ** (level + 1)) == 2 ** (level + 1) - 1)
+            def _():
+                store(incl.at[level], compose(arrived[level], held(level)[...]))
+
+    @pl.when(me == group - 1)
+    def _():
+        wait_state()
+        forward(held(levels - 1), group)
+
+    exclude(levels - 1, me, excl, arrived, upper)
+
+    @pl.when(jnp.logical_and(forwards, me >= group))
+    def _():
+        wait_state()
+        forward(held(levels), group)
 
     for item in down[-1:]:
         sweep(*item)
 
-    @pl.when(jnp.logical_not(jnp.logical_or(forwards, first_group)))
-    def _():
-        state_copy(0).wait_recv()
+    relays = forwards
+    for level in range(levels):
+        relays = jnp.logical_or(relays, me == 2**level - 1)
+
+    @pl.when(jnp.logical_not(relays))
+    def _():
+        wait_state()
 
     entry = jnp.sum(column(state[0:1, :]) * excl[:width, :], axis=0, keepdims=True)
     entry = entry + excl[width : width + 1, :]
@@ -316,10 +353,15 @@
         row_copy().wait_send()
 
     for level in range(levels):
-        @pl.when(sends(level))
+        @pl.when(jnp.logical_and(sends(level), me >= 2 ** (level + 1)))
         def _():
             for which in range(2**level):
                 map_copy(level, which).wait_send()
+
+        @pl.when(me == 2**level - 1)
+        def _():
+            for which in range(2**level):
+                state_copy(which).wait_send()
 
     @pl.when(forwards)
     def _():

time: 18.1 us -> 17.4 us (0.961)
  Pallas kernels: 16.5 us -> 15.7 us
    pallas_call x1, Pallas kernels: 16.5 us -> 15.7 us  [per_device(): pl.pallas_call(functools.partial(kernel, count, group), out_shape=jax.Sha...]
where the time goes in v3:
time: 17.4 us; the launch traced here: 17.1 us
  Pallas kernels  15.7 us (90%)
  local copies, waits for them, and re-layouts  1.38 us (8%)
    pallas_call x1, Pallas kernels, per_device(): pl.pallas_call(functools.partial(kernel, count, group), out_shape=jax.Sha...  15.7 us
    unnamed x1, local copies, waits for them, and re-layouts  1.38 us

profile of v3, /device:TPU:28, one launch (start us, length us, event | category | flops | bytes accessed | tf_op | source)
XLA Modules:
  0.0 17.1 jit_solution(17479120894968973682)
XLA Ops:
  0.0 15.7 %shard_map.64 = f32[64,128]{1,0:T(8,128)} custom-call(f32[64,128]{1,0:T(8,128)} %inputs_hbm.1, f32[64,128]{1,0:T(8,128)} %guesses_hbm.1, f32[128]{0:T(128)} %initial_hbm.1, f32[128,384]{1,0:T(8,128)} %w_input_hbm.1, f32[128,384]{1,0:T(8,128)} %w_hidden_hbm.1, f32[384]{0:T(512)} %biases_hbm.1), custom_call_target="tpu_custom_call" | custom-call | tf_op jit(solution)/shard_map/pallas_call | solution.py:381
  15.7 1.4 %copy.8 = f32[64,128]{1,0:T(8,128)} copy(f32[64,128]{1,0:T(8,128)} %shard_map.64) | data formatting | bytes 65536

commit v4 on v2

--- a/solution.py
+++ b/solution.py
@@ -1,5 +1,4 @@
 import functools
-import math
 
 import jax
 import jax.numpy as jnp
@@ -12,6 +11,7 @@
 SENT = 8
 BATCH = 4
 PAIRS = 3
+GROUP = 4
 
 
 def split(value):
@@ -59,46 +59,71 @@
     return update, coef_update, coef_reset, coef_cand, offset
 
 
+def store(ref, new):
+    width = new[0].shape[0]
+    ref[:width, :] = new[0]
+    ref[width:, :] = new[1]
+
+
 def kernel(
-    count, group,
+    count,
     inputs_hbm, guesses_hbm, initial_hbm, w_input_hbm, w_hidden_hbm, biases_hbm, out,
     inputs, initial, w_input, w_hidden, biases, packed,
     maps, prev, landed, pre_first, coefs, odd, arrived, incl, excl, state, state_next,
     load_sem, row_send, row_recv, map_send, map_recv, state_send, state_recv,
 ):
     steps, width = inputs.shape
-    levels = int(math.log2(group))
     me = lax.axis_index("seq")
-    place = lax.rem(me, group)
-    first_group = me < group
-    last_group = me >= count - group
-    leader = place == group - 1
-    forwards = jnp.logical_and(leader, jnp.logical_not(last_group))
-
-    def upper(level):
-        return lax.rem(lax.div(me, 2**level), 2) == 1
-
-    def sends(level):
-        return lax.rem(me, 2 ** (level + 1)) == 2**level - 1
+    plane, place = lax.div(me, GROUP), lax.rem(me, GROUP)
+    early_plane = plane == 0
+    late_plane = me >= count - GROUP
+    more = jnp.logical_not(late_plane)
+    later_plane = jnp.logical_not(early_plane)
+    odd_place = lax.rem(me, 2) == 1
+    far = place >= 2
+    both = jnp.logical_and
 
     def row_copy():
         return pltpu.make_async_remote_copy(
             src_ref=prev.at[pl.ds(steps, 8)], dst_ref=landed,
             send_sem=row_send, recv_sem=row_recv, device_id={"seq": me + 1})
 
-    def map_copy(level, which):
-        src = maps.at[steps // 2 - 1] if level == 0 else incl.at[level - 1]
+    def map_copy(src, slot, sem, device):
         return pltpu.make_async_remote_copy(
             src_ref=src.at[pl.ds(0, width + SENT)],
-            dst_ref=arrived.at[level, pl.ds(0, width + SENT)],
-            send_sem=map_send.at[2**level - 1 + which], recv_sem=map_recv.at[level],
-            device_id={"seq": me + 1 + which})
-
-    def state_copy(which):
+            dst_ref=arrived.at[slot, pl.ds(0, width + SENT)],
+            send_sem=map_send.at[sem], recv_sem=map_recv.at[slot],
+            device_id={"seq": device})
+
+    def state_copy(slot, which, device):
         return pltpu.make_async_remote_copy(
-            src_ref=state_next, dst_ref=state,
-            send_sem=state_send.at[which], recv_sem=state_recv,
-            device_id={"seq": me + 1 + which})
+            src_ref=state_next.at[slot], dst_ref=state,
+            send_sem=state_send.at[slot, which], recv_sem=state_recv,
+            device_id={"seq": device})
+
+    total = maps.at[steps // 2 - 1]
+    whole_pair = incl.at[0]
+    column_next = plane * GROUP + GROUP + jnp.where(far, 2, 0)
+    map_copies = [
+        (both(jnp.logical_not(odd_place), me > 0), [map_copy(total, 0, 0, me + 1)]),
+        (both(me == 2, more), [map_copy(total, 0, 1, 1)]),
+        (both(me == 3, more), [map_copy(total, 1, 0, 1)]),
+        (both(place == 1, later_plane),
+         [map_copy(whole_pair, 1, 0, me + 2), map_copy(whole_pair, 1, 1, me + 1)]),
+        (both(both(place == 3, later_plane), more), [map_copy(whole_pair, 1, 0, me - 2)]),
+    ]
+    state_copies = [
+        (me == 0, [state_copy(0, 0, 1)]),
+        (me == 1, [state_copy(0, 0, 3), state_copy(0, 1, 2)]),
+        (both(odd_place, more),
+         [state_copy(1, 0, column_next + 1), state_copy(1, 1, column_next)]),
+    ]
+
+    def start(entry):
+        @pl.when(entry[0])
+        def _():
+            for copy in entry[1]:
+                copy.start()
 
     loads = [
         pltpu.make_async_copy(src, dst, load_sem.at[k])
@@ -112,19 +137,18 @@
 
     barrier = pltpu.get_barrier_semaphore()
 
-    @pl.when(me > 0)
-    def _():
-        pl.semaphore_signal(barrier, 1, device_id={"seq": me - 1})
-
-    for level in range(levels):
-        @pl.when(upper(level))
+    def here(condition, device):
+        @pl.when(condition)
         def _():
-            source = lax.div(me, 2**level) * 2**level - 1
-            pl.semaphore_signal(barrier, 1, device_id={"seq": source})
-
-    @pl.when(jnp.logical_not(first_group))
-    def _():
-        pl.semaphore_signal(barrier, 1, device_id={"seq": lax.div(me, group) * group - 1})
+            pl.semaphore_signal(barrier, 1, device_id={"seq": device})
+
+    here(me > 0, me - 1)
+    here(odd_place, me - 1)
+    here(far, plane * GROUP + 1)
+    here(both(place == 1, more), me + 2)
+    here(both(me == 1, more), 2)
+    here(later_plane, plane * GROUP - jnp.where(far, 1, 3))
+    arrived[:, width + SENT :, :] = jnp.zeros((2, TAIL - SENT, width), jnp.float32)
 
     for load in loads:
         load.wait()
@@ -147,9 +171,9 @@
     for k, part in enumerate(gates(previous, pre, recurrent(previous))):
         coefs[k] = part
 
-    copies = 1 + group * forwards.astype(jnp.int32)
-    for level in range(levels):
-        copies += 2**level * sends(level).astype(jnp.int32)
+    copies = jnp.int32(1)
+    for condition, some in map_copies + state_copies:
+        copies += len(some) * condition.astype(jnp.int32)
 
     @pl.when(me < count - 1)
     def _():
@@ -171,10 +195,6 @@
         )
         return jnp.concatenate([body, jnp.where(top, off, 0.0)], axis=0)
 
-    def store(ref, new):
-        ref[:width, :] = new[0]
-        ref[width:, :] = new[1]
-
     def pair(i):
         store(maps.at[i], compose(step_map(2 * i), step_map(2 * i + 1)))
 
@@ -235,58 +255,95 @@
         down.append((3 * distance - 1, 2 * distance, distance, number // (2 * distance) - 1))
         distance //= 2
 
+    def applied(row, ref):
+        moved = jnp.sum(column(row) * ref[:width, :], axis=0, keepdims=True)
+        return moved + ref[width : width + 1, :]
+
+    def arrival(slot):
+        map_copy(total, slot, 0, me + 1).wait_recv()
+
+    def wait_state():
+        state_copy(0, 0, me + 1).wait_recv()
+
+    @pl.when(me == 0)
+    def _():
+        state[...] = jnp.broadcast_to(initial[...][None, :], state.shape)
+        state_next[0] = jnp.broadcast_to(applied(state[0:1, :], total), (8, width))
+
+    start(state_copies[0])
+    for entry in map_copies[:3]:
+        start(entry)
     excl[:width, :] = jnp.where(rows == cols, 1.0, 0.0)
     excl[width:, :] = jnp.zeros((TAIL, width), jnp.float32)
-    share = {0: down[:-1]}
-    for level in range(levels):
-        @pl.when(sends(level))
-        def _():
-            for which in range(2**level):
-                map_copy(level, 2**level - 1 - which).start()
-
-        for item in share.get(level, ()):
-            sweep(*item)
-
-        held = maps.at[number - 1] if level == 0 else incl.at[level - 1]
-
-        @pl.when(upper(level))
-        def _():
-            map_copy(level, 0).wait_recv()
-            arrived[level, pl.ds(width + SENT, TAIL - SENT), :] = jnp.zeros(
-                (TAIL - SENT, width), jnp.float32)
-            early = arrived[level]
-            store(incl.at[level], compose(early, held[...]))
-            store(excl, compose(early, excl[...]))
-
-        @pl.when(jnp.logical_not(upper(level)))
-        def _():
-            incl[level] = held[...]
-
-    @pl.when(first_group)
-    def _():
-        state[...] = jnp.broadcast_to(initial[...][None, :], state.shape)
-
-    @pl.when(forwards)
-    def _():
-        @pl.when(jnp.logical_not(first_group))
-        def _():
-            state_copy(0).wait_recv()
-        whole = incl.at[levels - 1]
-        moved = jnp.sum(column(state[0:1, :]) * whole[:width, :], axis=0, keepdims=True)
-        state_next[...] = jnp.broadcast_to(
-            moved + whole[width : width + 1, :], state_next.shape)
-        for which in range(group):
-            state_copy(group - 1 - which).start()
+    for item in down[:-2]:
+        sweep(*item)
+
+    @pl.when(me == 1)
+    def _():
+        wait_state()
+        state_next[0] = jnp.broadcast_to(applied(state[0:1, :], total), (8, width))
+
+    start(state_copies[1])
+
+    @pl.when(both(odd_place, me >= 3))
+    def _():
+        arrival(0)
+        store(incl.at[0], compose(arrived[0], total[...]))
+        excl[...] = arrived[0]
+
+    for entry in map_copies[3:]:
+        start(entry)
+    for item in down[-2:-1]:
+        sweep(*item)
+
+    @pl.when(both(me == 1, more))
+    def _():
+        arrival(0)
+        arrival(1)
+        state_next[1] = jnp.broadcast_to(
+            applied(applied(state_next[0, 0:1, :], arrived.at[0]), arrived.at[1]), (8, width))
+
+    @pl.when(me == 3)
+    def _():
+        wait_state()
+        state_next[1] = jnp.broadcast_to(applied(state[0:1, :], whole_pair), (8, width))
+
+    @pl.when(both(later_plane, jnp.logical_or(far, both(place == 1, more))))
+    def _():
+        arrival(1)
+
+    @pl.when(both(both(later_plane, more), place == 1))
+    def _():
+        store(incl.at[1], compose(incl[0], arrived[1]))
+
+    @pl.when(both(both(later_plane, more), place == 3))
+    def _():
+        store(incl.at[1], compose(arrived[1], incl[0]))
+
+    @pl.when(both(both(later_plane, more), odd_place))
+    def _():
+        wait_state()
+        state_next[1] = jnp.broadcast_to(applied(state[0:1, :], incl.at[1]), (8, width))
+
+    start(state_copies[2])
+
+    @pl.when(both(later_plane, place == 2))
+    def _():
+        excl[...] = arrived[1]
+
+    @pl.when(both(later_plane, place == 3))
+    def _():
+        store(excl, compose(arrived[1], arrived[0]))
 
     for item in down[-1:]:
         sweep(*item)
 
-    @pl.when(jnp.logical_not(jnp.logical_or(forwards, first_group)))
-    def _():
-        state_copy(0).wait_recv()
-
-    entry = jnp.sum(column(state[0:1, :]) * excl[:width, :], axis=0, keepdims=True)
-    entry = entry + excl[width : width + 1, :]
+    @pl.when(jnp.logical_or(
+        me == 2, both(later_plane, jnp.logical_or(late_plane, jnp.logical_not(odd_place)))))
+    def _():
+        wait_state()
+
+    entry = applied(state[0:1, :], excl)
     across = column(entry)
     odd[0:8, :] = jnp.broadcast_to(entry, (8, width))
 
@@ -315,29 +372,22 @@
     def _():
         row_copy().wait_send()
 
-    for level in range(levels):
-        @pl.when(sends(level))
+    for condition, some in map_copies + state_copies:
+        @pl.when(condition)
         def _():
-            for which in range(2**level):
-                map_copy(level, which).wait_send()
-
-    @pl.when(forwards)
-    def _():
-        for which in range(group):
-            state_copy(which).wait_send()
+            for copy in some:
+                copy.wait_send()
 
 
 def solution(mesh):
     count = mesh.shape["seq"]
-    group = 4
 
     def per_device(inputs, guesses, initial, w_input, w_hidden, biases):
         steps, width = guesses.shape
-        levels = int(math.log2(group))
         full = width + TAIL
         line = pltpu.VMEM((steps, width), jnp.float32)
         return pl.pallas_call(
-            functools.partial(kernel, count, group),
+            functools.partial(kernel, count),
             out_shape=jax.ShapeDtypeStruct((steps, width), jnp.float32),
             in_specs=[pl.BlockSpec(memory_space=pl.ANY)] * 6,
             out_specs=pl.BlockSpec(memory_space=pltpu.VMEM),
@@ -354,17 +404,17 @@
                 pltpu.VMEM((16, 3 * width), jnp.float32),
                 pltpu.VMEM((5, steps, width), jnp.float32),
                 pltpu.VMEM((steps // 2 + 8, width), jnp.float32),
-                pltpu.VMEM((levels, full, width), jnp.float32),
-                pltpu.VMEM((levels, full, width), jnp.float32),
+                pltpu.VMEM((2, full, width), jnp.float32),
+                pltpu.VMEM((2, full, width), jnp.float32),
                 pltpu.VMEM((full, width), jnp.float32),
                 pltpu.VMEM((8, width), jnp.float32),
-                pltpu.VMEM((8, width), jnp.float32),
+                pltpu.VMEM((2, 8, width), jnp.float32),
                 pltpu.SemaphoreType.DMA((6,)),
                 pltpu.SemaphoreType.DMA,
                 pltpu.SemaphoreType.DMA,
-                pltpu.SemaphoreType.DMA((group - 1,)),
-                pltpu.SemaphoreType.DMA((levels,)),
-                pltpu.SemaphoreType.DMA((group,)),
+                pltpu.SemaphoreType.DMA((2,)),
+                pltpu.SemaphoreType.DMA((2,)),
+                pltpu.SemaphoreType.DMA((2, 2)),
                 pltpu.SemaphoreType.DMA,
             ],
             compiler_params=pltpu.CompilerParams(

time: 18.1 us -> 17.8 us (0.983)
  Pallas kernels: 16.5 us -> 16.2 us
    pallas_call x1, Pallas kernels: 16.5 us -> 16.2 us  [per_device(): pl.pallas_call(functools.partial(kernel, count), out_shape=jax.ShapeDtype...]
where the time goes in v4:
time: 17.8 us; the launch traced here: 17.6 us
  Pallas kernels  16.2 us (91%)
  local copies, waits for them, and re-layouts  1.38 us (8%)
    pallas_call x1, Pallas kernels, per_device(): pl.pallas_call(functools.partial(kernel, count), out_shape=jax.ShapeDtype...  16.2 us
    unnamed x1, local copies, waits for them, and re-layouts  1.38 us

profile of v4, /device:TPU:28, one launch (start us, length us, event | category | flops | bytes accessed | tf_op | source)
XLA Modules:
  0.0 17.6 jit_solution(18154912478651084276)
XLA Ops:
  0.0 16.2 %shard_map.64 = f32[64,128]{1,0:T(8,128)} custom-call(f32[64,128]{1,0:T(8,128)} %inputs_hbm.1, f32[64,128]{1,0:T(8,128)} %guesses_hbm.1, f32[128]{0:T(128)} %initial_hbm.1, f32[128,384]{1,0:T(8,128)} %w_input_hbm.1, f32[128,384]{1,0:T(8,128)} %w_hidden_hbm.1, f32[384]{0:T(512)} %biases_hbm.1), custom_call_target="tpu_custom_call" | custom-call | tf_op jit(solution)/shard_map/pallas_call | solution.py:389
  16.2 1.4 %copy.8 = f32[64,128]{1,0:T(8,128)} copy(f32[64,128]{1,0:T(8,128)} %shard_map.64) | data formatting | bytes 65536

commit v5 on v4

--- a/solution.py
+++ b/solution.py
@@ -9,8 +9,8 @@
 
 TAIL = 16
 SENT = 8
-BATCH = 4
-PAIRS = 3
+BATCH = 16
+PAIRS = 8
 GROUP = 4
 
 
@@ -106,8 +106,6 @@
     column_next = plane * GROUP + GROUP + jnp.where(far, 2, 0)
     map_copies = [
         (both(jnp.logical_not(odd_place), me > 0), [map_copy(total, 0, 0, me + 1)]),
-        (both(me == 2, more), [map_copy(total, 0, 1, 1)]),
-        (both(me == 3, more), [map_copy(total, 1, 0, 1)]),
         (both(place == 1, later_plane),
          [map_copy(whole_pair, 1, 0, me + 2), map_copy(whole_pair, 1, 1, me + 1)]),
         (both(both(place == 3, later_plane), more), [map_copy(whole_pair, 1, 0, me - 2)]),
@@ -115,8 +113,9 @@
     state_copies = [
         (me == 0, [state_copy(0, 0, 1)]),
         (me == 1, [state_copy(0, 0, 3), state_copy(0, 1, 2)]),
-        (both(odd_place, more),
+        (both(both(odd_place, more), me >= 3),
          [state_copy(1, 0, column_next + 1), state_copy(1, 1, column_next)]),
+        (both(me == 3, more), [state_copy(1, 2, GROUP), state_copy(1, 3, GROUP + 1)]),
     ]
 
     def start(entry):
@@ -128,9 +127,9 @@
     loads = [
         pltpu.make_async_copy(src, dst, load_sem.at[k])
         for k, (src, dst) in enumerate([
-            (w_hidden_hbm, w_hidden), (w_input_hbm, w_input),
-            (guesses_hbm, prev.at[pl.ds(8, steps)]), (inputs_hbm, inputs),
-            (initial_hbm, initial), (biases_hbm, biases)])
+            (guesses_hbm, prev.at[pl.ds(8, steps)]), (initial_hbm, initial),
+            (w_hidden_hbm, w_hidden), (inputs_hbm, inputs),
+            (w_input_hbm, w_input), (biases_hbm, biases)])
     ]
     for load in loads:
         load.start()
@@ -145,12 +144,11 @@
     here(me > 0, me - 1)
     here(odd_place, me - 1)
     here(far, plane * GROUP + 1)
-    here(both(place == 1, more), me + 2)
-    here(both(me == 1, more), 2)
-    here(later_plane, plane * GROUP - jnp.where(far, 1, 3))
+    here(both(both(place == 1, later_plane), more), me + 2)
+    here(later_plane, plane * GROUP - jnp.where(jnp.logical_or(far, plane == 1), 1, 3))
     arrived[:, width + SENT :, :] = jnp.zeros((2, TAIL - SENT, width), jnp.float32)
 
-    for load in loads:
+    for load in loads[:3]:
         load.wait()
 
     prev[pl.ds(0, 8), :] = jnp.broadcast_to(initial[...][None, :], (8, width))
@@ -165,10 +163,13 @@
             preferred_element_type=jnp.float32)
         return both[:, : 3 * width] + both[:, 3 * width :]
 
+    previous = prev[pl.ds(7, steps), :]
+    rec = recurrent(previous)
+    for load in loads[3:]:
+        load.wait()
     pre = product(inputs[...], w_input[...]) + biases[...][None, :]
     pre_first[...] = pre[:16]
-    previous = prev[pl.ds(7, steps), :]
-    for k, part in enumerate(gates(previous, pre, recurrent(previous))):
+    for k, part in enumerate(gates(previous, pre, rec)):
         coefs[k] = part
 
     copies = jnp.int32(1)
@@ -195,9 +196,6 @@
         )
         return jnp.concatenate([body, jnp.where(top, off, 0.0)], axis=0)
 
-    def pair(i):
-        store(maps.at[i], compose(step_map(2 * i), step_map(2 * i + 1)))
-
     def pairs(start, size):
         news = [compose(step_map(2 * i), step_map(2 * i + 1))
                 for i in [start + k for k in range(size)]]
@@ -205,12 +203,11 @@
             store(maps.at[start + k], new)
 
     def pairs_body(j, _):
-        pairs(1 + PAIRS * j, PAIRS)
+        pairs(PAIRS * j, PAIRS)
         return 0
 
     number = steps // 2
-    whole = (number - 1) // PAIRS
-    lax.fori_loop(0, whole, pairs_body, 0)
+    lax.fori_loop(1, number // PAIRS, pairs_body, 0)
 
     @pl.when(me > 0)
     def _():
@@ -220,8 +217,7 @@
         for k, part in enumerate(gates(fixed, pre_first[...], recurrent(fixed))):
             coefs[k, :16, :] = part
 
-    for i in [0] + list(range(1 + PAIRS * whole, number)):
-        pair(i)
+    pairs(0, PAIRS)
 
     def sweep(first, stride, distance, number):
         batch = min(BATCH, number)
@@ -271,8 +267,7 @@
         state_next[0] = jnp.broadcast_to(applied(state[0:1, :], total), (8, width))
 
     start(state_copies[0])
-    for entry in map_copies[:3]:
-        start(entry)
+    start(map_copies[0])
     excl[:width, :] = jnp.where(rows == cols, 1.0, 0.0)
     excl[width:, :] = jnp.zeros((TAIL, width), jnp.float32)
     for item in down[:-2]:
@@ -291,18 +286,11 @@
         store(incl.at[0], compose(arrived[0], total[...]))
         excl[...] = arrived[0]
 
-    for entry in map_copies[3:]:
+    for entry in map_copies[1:]:
         start(entry)
     for item in down[-2:-1]:
         sweep(*item)
 
-    @pl.when(both(me == 1, more))
-    def _():
-        arrival(0)
-        arrival(1)
-        state_next[1] = jnp.broadcast_to(
-            applied(applied(state_next[0, 0:1, :], arrived.at[0]), arrived.at[1]), (8, width))
-
     @pl.when(me == 3)
     def _():
         wait_state()
@@ -326,6 +314,7 @@
         state_next[1] = jnp.broadcast_to(applied(state[0:1, :], incl.at[1]), (8, width))
 
     start(state_copies[2])
+    start(state_copies[3])
 
     @pl.when(both(later_plane, place == 2))
     def _():
@@ -414,7 +403,7 @@
                 pltpu.SemaphoreType.DMA,
                 pltpu.SemaphoreType.DMA((2,)),
                 pltpu.SemaphoreType.DMA((2,)),
-                pltpu.SemaphoreType.DMA((2, 2)),
+                pltpu.SemaphoreType.DMA((2, 4)),
                 pltpu.SemaphoreType.DMA,
             ],
             compiler_params=pltpu.CompilerParams(

time: 17.8 us -> 15.6 us (0.88)
  Pallas kernels: 16.2 us -> 14 us
    pallas_call x1, Pallas kernels: 16.2 us -> 14 us  [per_device(): pl.pallas_call(functools.partial(kernel, count), out_shape=jax.ShapeDtype...]
where the time goes in v5:
time: 15.6 us; the launch traced here: 15.4 us
  Pallas kernels  14 us (90%)
  local copies, waits for them, and re-layouts  1.38 us (9%)
    pallas_call x1, Pallas kernels, per_device(): pl.pallas_call(functools.partial(kernel, count), out_shape=jax.ShapeDtype...  14 us
    unnamed x1, local copies, waits for them, and re-layouts  1.38 us

profile of v5, /device:TPU:28, one launch (start us, length us, event | category | flops | bytes accessed | tf_op | source)
XLA Modules:
  0.0 15.4 jit_solution(13094543563921081570)
XLA Ops:
  0.0 14.0 %shard_map.64 = f32[64,128]{1,0:T(8,128)} custom-call(f32[64,128]{1,0:T(8,128)} %inputs_hbm.1, f32[64,128]{1,0:T(8,128)} %guesses_hbm.1, f32[128]{0:T(128)} %initial_hbm.1, f32[128,384]{1,0:T(8,128)} %w_input_hbm.1, f32[128,384]{1,0:T(8,128)} %w_hidden_hbm.1, f32[384]{0:T(512)} %biases_hbm.1), custom_call_target="tpu_custom_call" | custom-call | tf_op jit(solution)/shard_map/pallas_call | solution.py:378
  14.0 1.4 %copy.8 = f32[64,128]{1,0:T(8,128)} copy(f32[64,128]{1,0:T(8,128)} %shard_map.64) | data formatting | bytes 65536

commit v6 on v5

--- a/solution.py
+++ b/solution.py
@@ -107,8 +107,9 @@
     map_copies = [
         (both(jnp.logical_not(odd_place), me > 0), [map_copy(total, 0, 0, me + 1)]),
         (both(place == 1, later_plane),
-         [map_copy(whole_pair, 1, 0, me + 2), map_copy(whole_pair, 1, 1, me + 1)]),
+         [map_copy(whole_pair, 1, 0, me + 2)]),
         (both(both(place == 3, later_plane), more), [map_copy(whole_pair, 1, 0, me - 2)]),
+        (both(place == 3, later_plane), [map_copy(arrived.at[1], 1, 1, me - 1)]),
     ]
     state_copies = [
         (me == 0, [state_copy(0, 0, 1)]),
@@ -143,7 +144,7 @@
 
     here(me > 0, me - 1)
     here(odd_place, me - 1)
-    here(far, plane * GROUP + 1)
+    here(far, plane * GROUP + jnp.where(both(later_plane, place == 2), 3, 1))
     here(both(both(place == 1, later_plane), more), me + 2)
     here(later_plane, plane * GROUP - jnp.where(jnp.logical_or(far, plane == 1), 1, 3))
     arrived[:, width + SENT :, :] = jnp.zeros((2, TAIL - SENT, width), jnp.float32)
@@ -172,13 +173,14 @@
     for k, part in enumerate(gates(previous, pre, rec)):
         coefs[k] = part
 
-    copies = jnp.int32(1)
+    copies = (me < count - 1).astype(jnp.int32)
     for condition, some in map_copies + state_copies:
         copies += len(some) * condition.astype(jnp.int32)
 
+    pl.semaphore_wait(barrier, copies)
+
     @pl.when(me < count - 1)
     def _():
-        pl.semaphore_wait(barrier, copies)
         row_copy().start()
 
     rows = lax.broadcasted_iota(jnp.int32, (width, width), 0)
@@ -202,12 +204,9 @@
         for k, new in enumerate(news):
             store(maps.at[start + k], new)
 
-    def pairs_body(j, _):
-        pairs(PAIRS * j, PAIRS)
-        return 0
-
     number = steps // 2
-    lax.fori_loop(1, number // PAIRS, pairs_body, 0)
+    for k in range(2):
+        pairs(PAIRS + k * (number - PAIRS) // 2, (number - PAIRS) // 2)
 
     @pl.when(me > 0)
     def _():
@@ -286,7 +285,7 @@
         store(incl.at[0], compose(arrived[0], total[...]))
         excl[...] = arrived[0]
 
-    for entry in map_copies[1:]:
+    for entry in map_copies[1:3]:
         start(entry)
     for item in down[-2:-1]:
         sweep(*item)
@@ -300,15 +299,24 @@
     def _():
         arrival(1)
 
+    start(map_copies[3])
+    second = both(both(plane == 1, more), place == 3)
+
     @pl.when(both(both(later_plane, more), place == 1))
     def _():
         store(incl.at[1], compose(incl[0], arrived[1]))
 
-    @pl.when(both(both(later_plane, more), place == 3))
+    @pl.when(both(both(plane > 1, more), place == 3))
     def _():
         store(incl.at[1], compose(arrived[1], incl[0]))
 
-    @pl.when(both(both(later_plane, more), odd_place))
+    @pl.when(second)
+    def _():
+        wait_state()
+        row = applied(applied(state[0:1, :], arrived.at[1]), whole_pair)
+        state_next[1] = jnp.broadcast_to(row, (8, width))
+
+    @pl.when(both(both(both(later_plane, more), odd_place), jnp.logical_not(second)))
     def _():
         wait_state()
         state_next[1] = jnp.broadcast_to(applied(state[0:1, :], incl.at[1]), (8, width))
@@ -336,16 +344,12 @@
     across = column(entry)
     odd[0:8, :] = jnp.broadcast_to(entry, (8, width))
 
-    def finish(j, _):
+    for j in range(0, number, 8):
         lines = []
-        for k in range(8):
-            i = j * 8 + k
+        for i in range(j, j + 8):
             line = jnp.sum(across * maps[i, :width, :], axis=0, keepdims=True)
             lines.append(line + maps[i, width : width + 1, :])
-        odd[pl.ds(pl.multiple_of(8 + j * 8, 8), 8), :] = jnp.concatenate(lines, axis=0)
-        return 0
-
-    lax.fori_loop(0, number // 8, finish, 0)
+        odd[j + 8 : j + 16, :] = jnp.concatenate(lines, axis=0)
 
     before = odd[pl.ds(7, number), :]
     rec = recurrent(before)

time: 15.6 us -> 15.4 us (0.987)
  Pallas kernels: 14 us -> 13.8 us
where the time goes in v6:
time: 15.4 us; the launch traced here: 15.2 us
  Pallas kernels  13.8 us (90%)
  local copies, waits for them, and re-layouts  1.38 us (9%)
    pallas_call x1, Pallas kernels, per_device(): pl.pallas_call(functools.partial(kernel, count), out_shape=jax.ShapeDtype...  13.8 us
    unnamed x1, local copies, waits for them, and re-layouts  1.38 us

profile of v6, /device:TPU:28, one launch (start us, length us, event | category | flops | bytes accessed | tf_op | source)
XLA Modules:
  0.0 15.2 jit_solution(11631824515255664308)
XLA Ops:
  0.0 13.8 %shard_map.64 = f32[64,128]{1,0:T(8,128)} custom-call(f32[64,128]{1,0:T(8,128)} %inputs_hbm.1, f32[64,128]{1,0:T(8,128)} %guesses_hbm.1, f32[128]{0:T(128)} %initial_hbm.1, f32[128,384]{1,0:T(8,128)} %w_input_hbm.1, f32[128,384]{1,0:T(8,128)} %w_hidden_hbm.1, f32[384]{0:T(512)} %biases_hbm.1), custom_call_target="tpu_custom_call" | custom-call | tf_op jit(solution)/shard_map/pallas_call | solution.py:382
  13.8 1.4 %copy.8 = f32[64,128]{1,0:T(8,128)} copy(f32[64,128]{1,0:T(8,128)} %shard_map.64) | data formatting | bytes 65536

commit v7 on v6

--- a/solution.py
+++ b/solution.py
@@ -170,9 +170,6 @@
         load.wait()
     pre = product(inputs[...], w_input[...]) + biases[...][None, :]
     pre_first[...] = pre[:16]
-    for k, part in enumerate(gates(previous, pre, rec)):
-        coefs[k] = part
-
     copies = (me < count - 1).astype(jnp.int32)
     for condition, some in map_copies + state_copies:
         copies += len(some) * condition.astype(jnp.int32)
@@ -182,6 +179,9 @@
     @pl.when(me < count - 1)
     def _():
         row_copy().start()
+
+    for k, part in enumerate(gates(previous, pre, rec)):
+        coefs[k] = part
 
     rows = lax.broadcasted_iota(jnp.int32, (width, width), 0)
     cols = lax.broadcasted_iota(jnp.int32, (width, width), 1)
@@ -205,17 +205,19 @@
             store(maps.at[start + k], new)
 
     number = steps // 2
-    for k in range(2):
-        pairs(PAIRS + k * (number - PAIRS) // 2, (number - PAIRS) // 2)
+    half = (number + PAIRS) // 2
+    pairs(PAIRS, half - PAIRS)
 
     @pl.when(me > 0)
     def _():
         row_copy().wait_recv()
         prev[pl.ds(7, 1), :] = landed[pl.ds(7, 1), :]
-        fixed = prev[pl.ds(7, 16), :]
-        for k, part in enumerate(gates(fixed, pre_first[...], recurrent(fixed))):
-            coefs[k, :16, :] = part
-
+
+    fixed = prev[pl.ds(7, 16), :]
+    parts = gates(fixed, pre_first[...], recurrent(fixed))
+    pairs(half, number - half)
+    for k, part in enumerate(parts):
+        coefs[k, :16, :] = part
     pairs(0, PAIRS)
 
     def sweep(first, stride, distance, number):
@@ -372,6 +374,12 @@
                 copy.wait_send()
 
 
+def moved_out(src, dst, sem):
+    copy = pltpu.make_async_copy(src, dst, sem)
+    copy.start()
+    copy.wait()
+
+
 def solution(mesh):
     count = mesh.shape["seq"]
 
@@ -379,7 +387,7 @@
         steps, width = guesses.shape
         full = width + TAIL
         line = pltpu.VMEM((steps, width), jnp.float32)
-        return pl.pallas_call(
+        rows = pl.pallas_call(
             functools.partial(kernel, count),
             out_shape=jax.ShapeDtypeStruct((steps, width), jnp.float32),
             in_specs=[pl.BlockSpec(memory_space=pl.ANY)] * 6,
@@ -413,6 +421,14 @@
             compiler_params=pltpu.CompilerParams(
                 collective_id=0, has_side_effects=True, vmem_limit_bytes=56 * 2**20),
         )(inputs, guesses, initial, w_input, w_hidden, biases)
+        return pl.pallas_call(
+            moved_out,
+            out_shape=jax.ShapeDtypeStruct((steps, width), jnp.float32),
+            in_specs=[pl.BlockSpec(memory_space=pl.ANY)],
+            out_specs=pl.BlockSpec(memory_space=pl.ANY),
+            scratch_shapes=[pltpu.SemaphoreType.DMA],
+            compiler_params=pltpu.CompilerParams(vmem_limit_bytes=56 * 2**20),
+        )(rows)
 
     placed = (P(("groups", "seq"), None), P(("groups", "seq"), None), P("groups"), P(), P(), P())
     return jax.shard_map(

time: 15.4 us -> 16.4 us (1.065)
  Pallas kernels: 13.8 us -> 16.2 us
  local copies, waits for them, and re-layouts: 1.38 us -> 0 us
    pallas_call x0 -> x1, Pallas kernels: none -> 2.1 us  [per_device(): pl.pallas_call(moved_out, out_shape=jax.ShapeDtypeStruct((steps, width),...]
    unnamed x1 -> x0, local copies, waits for them, and re-layouts: 1.38 us -> none
    pallas_call x1, Pallas kernels: 13.8 us -> 14.1 us  [per_device(): pl.pallas_call(functools.partial(kernel, count), out_shape=jax.ShapeDtype...]
where the time goes in v7:
time: 16.4 us; the launch traced here: 16.3 us
  Pallas kernels  16.2 us (99%)
    pallas_call x1, Pallas kernels, per_device(): pl.pallas_call(functools.partial(kernel, count), out_shape=jax.ShapeDtype...  14.1 us
    pallas_call x1, Pallas kernels, per_device(): pl.pallas_call(moved_out, out_shape=jax.ShapeDtypeStruct((steps, width),...  2.1 us

profile of v7, /device:TPU:28, one launch (start us, length us, event | category | flops | bytes accessed | tf_op | source)
XLA Modules:
  0.0 16.3 jit_solution(2031434206715489844)
XLA Ops:
  0.0 14.1 %shard_map.64.src = f32[64,128]{1,0:T(8,128)} custom-call(f32[64,128]{1,0:T(8,128)} %inputs_hbm.1, f32[64,128]{1,0:T(8,128)} %guesses_hbm.1, f32[128]{0:T(128)} %initial_hbm.1, f32[128,384]{1,0:T(8,128)} %w_input_hbm.1, f32[128,384]{1,0:T(8,128)} %w_hidden_hbm.1, f32[384]{0:T(512)} %biases_hbm.1), custom_call_target="tpu_custom_call" | custom-call | tf_op jit(solution)/shard_map/pallas_call | solution.py:390
  14.2 2.1 %shard_map.65 = f32[64,128]{1,0:T(8,128)} custom-call(f32[64,128]{1,0:T(8,128)} %shard_map.64.src), custom_call_target="tpu_custom_call" | custom-call | tf_op jit(solution)/shard_map/pallas_call | solution.py:424

commit v8 on v6

--- a/solution.py
+++ b/solution.py
@@ -300,9 +300,9 @@
         arrival(1)
 
     start(map_copies[3])
-    second = both(both(plane == 1, more), place == 3)
-
-    @pl.when(both(both(later_plane, more), place == 1))
+    second = both(both(plane == 1, more), odd_place)
+
+    @pl.when(both(both(plane > 1, more), place == 1))
     def _():
         store(incl.at[1], compose(incl[0], arrived[1]))
 
@@ -310,7 +310,13 @@
     def _():
         store(incl.at[1], compose(arrived[1], incl[0]))
 
-    @pl.when(second)
+    @pl.when(both(second, place == 1))
+    def _():
+        wait_state()
+        row = applied(applied(state[0:1, :], whole_pair), arrived.at[1])
+        state_next[1] = jnp.broadcast_to(row, (8, width))
+
+    @pl.when(both(second, place == 3))
     def _():
         wait_state()
         row = applied(applied(state[0:1, :], arrived.at[1]), whole_pair)
@@ -321,8 +327,8 @@
         wait_state()
         state_next[1] = jnp.broadcast_to(applied(state[0:1, :], incl.at[1]), (8, width))
 
+    start(state_copies[3])
     start(state_copies[2])
-    start(state_copies[3])
 
     @pl.when(both(later_plane, place == 2))
     def _():

time: 15.4 us -> 15.3 us (level)
  no operation moved by 1% of the time
where the time goes in v8:
time: 15.3 us; the launch traced here: 15.2 us
  Pallas kernels  13.8 us (90%)
  local copies, waits for them, and re-layouts  1.38 us (9%)
    pallas_call x1, Pallas kernels, per_device(): pl.pallas_call(functools.partial(kernel, count), out_shape=jax.ShapeDtype...  13.8 us
    unnamed x1, local copies, waits for them, and re-layouts  1.38 us

profile of v8, /device:TPU:28, one launch (start us, length us, event | category | flops | bytes accessed | tf_op | source)
XLA Modules:
  0.0 15.2 jit_solution(14625731497315326923)
XLA Ops:
  0.0 13.8 %shard_map.64 = f32[64,128]{1,0:T(8,128)} custom-call(f32[64,128]{1,0:T(8,128)} %inputs_hbm.1, f32[64,128]{1,0:T(8,128)} %guesses_hbm.1, f32[128]{0:T(128)} %initial_hbm.1, f32[128,384]{1,0:T(8,128)} %w_input_hbm.1, f32[128,384]{1,0:T(8,128)} %w_hidden_hbm.1, f32[384]{0:T(512)} %biases_hbm.1), custom_call_target="tpu_custom_call" | custom-call | tf_op jit(solution)/shard_map/pallas_call | solution.py:388
  13.8 1.4 %copy.8 = f32[64,128]{1,0:T(8,128)} copy(f32[64,128]{1,0:T(8,128)} %shard_map.64) | data formatting | bytes 65536
